TPU v7x, 256 devices: a whole 4x4x8 slice. The times are simulated.
256 devices in a mesh: sector: 16 (over x_lo, z), band: 16 (over x_hi, y, core).
Axes of the slice: x: 4 (x_hi: 2, x_lo: 2; x = x_hi * 2 + x_lo), y: 4, z: 8, core: 2. Of those that a mesh axis runs over, the one named last changes fastest.
Arguments:
- queries: bfloat16 [256, 1024, 256], P('sector', 'band'), may hold values from -6 to 6
- norm_gain: float32 [256], replicated, may hold values from 0.5 to 1.5
- w_query: bfloat16 [256, 256], replicated, may hold values from -0.375 to 0.375
- w_key: bfloat16 [256, 256], replicated, may hold values from -0.375 to 0.375
- w_value: bfloat16 [256, 256], replicated, may hold values from -0.375 to 0.375
- w_out: bfloat16 [256, 256], replicated, may hold values from -0.375 to 0.375
- features: bfloat16 [131072, 256], P(('sector', 'band')), may hold values from -160 to 160
- visible: int32 [256, 1024, 3], P('sector', 'band'), may hold values from 0 to 3071, as said below
- live: int32 [256, 1024, 3], P('sector', 'band'), may hold values from 0 to 1, as said below
Outputs:
- attended: bfloat16 [256, 1024, 256], P('sector', 'band')
Inputs may be any that keep to these rules, and one draw needn't show every extreme that they name: `visible`: on each device (s, j), the 3072 entries name every code from 0 to 3071 exactly once. `live`: 1 marks an entry that contributes, 0 one that does not.
All inputs are finite; a program needn't handle non-finite values.
Results may differ from a plain program's by a relative error of at most 0.0025.
The roundings to bfloat16 on the way count: a program that leaves them out, or rounds other values in their place, can miss the bound.
Values may be sent and summed in bfloat16 or wider, within the bound.
A program may use at most 128 MiB of HBM per device.

v0:
```python
import jax
import jax.numpy as jnp
from jax import lax
from jax.sharding import PartitionSpec as P

HEADS = 8
BLK_DEV = 8
CAP = 128


def passed_along(block, axis, distance):
    devices = range(lax.axis_size(axis))
    route = [((i - distance) % len(devices), i) for i in devices]
    return lax.ppermute(block, axis, route)


def attend_pair(rows, blocks):
    pair_count, row_count, model_width = rows.shape
    key_count = blocks.shape[1]
    head_size = model_width // HEADS
    query_heads = rows.reshape(pair_count, row_count, HEADS, head_size)
    key_heads = blocks[:, :, :model_width].reshape(pair_count, key_count, HEADS, head_size)
    value_heads = blocks[:, :, model_width:].reshape(pair_count, key_count, HEADS, head_size)
    scores = jnp.einsum(
        "bmhd,bkhd->bhmk", query_heads, key_heads, preferred_element_type=jnp.float32
    ) * head_size ** (-0.5)
    peak = jnp.max(scores, axis=-1, keepdims=True)
    expo = jnp.exp(scores - peak)
    weights = (expo / jnp.sum(expo, axis=-1, keepdims=True)).astype(jnp.bfloat16)
    heads_out = jnp.einsum(
        "bhmk,bkhd->bmhd", weights, value_heads, preferred_element_type=jnp.float32
    )
    return heads_out.astype(jnp.bfloat16).reshape(pair_count, row_count, model_width)


def attend_many(rows, blocks):
    block_count = rows.shape[0]
    pair_size = 2
    grouped_rows = rows.reshape((block_count // pair_size, pair_size) + rows.shape[1:])
    grouped_blocks = blocks.reshape((block_count // pair_size, pair_size) + blocks.shape[1:])
    result = lax.map(lambda pair: attend_pair(pair[0], pair[1]), (grouped_rows, grouped_blocks))
    return result.reshape(rows.shape)


def attend_groups(query_groups, kv_groups):
    model_width = query_groups.shape[3]
    group_count = kv_groups.shape[0]
    outputs = []
    for group in range(3):
        kv_blocks = kv_groups[min(group, group_count - 1)].reshape(BLK_DEV, -1, 2 * model_width)
        outputs.append(attend_many(query_groups[group], kv_blocks))
    return jnp.stack(outputs, axis=0)


def shards(queries, norm_gain, w_query, w_key, w_value, w_out, features, visible, live):
    azim_cells, range_cells, model_width = queries.shape
    entries = visible.shape[2]
    query_count = azim_cells * range_cells
    values_in = queries.reshape(query_count, model_width).astype(jnp.float32)
    average = jnp.mean(values_in, axis=-1, keepdims=True)
    spread = jnp.mean((values_in - average) ** 2, axis=-1, keepdims=True)
    normed = ((values_in - average) * lax.rsqrt(spread + 1e-05) * norm_gain).astype(jnp.bfloat16)
    projected = jnp.dot(normed, w_query, preferred_element_type=jnp.float32).astype(jnp.bfloat16)
    slot_codes = visible.reshape(-1)
    slot_total = 3 * BLK_DEV * CAP
    slots = (
        jnp.zeros((slot_total, model_width), jnp.bfloat16)
        .at[slot_codes]
        .set(jnp.repeat(projected, entries, axis=0))
    )
    slots = slots.reshape(3, BLK_DEV, CAP, model_width)
    w_both = jnp.concatenate([w_key, w_value], axis=1)
    local_kv = jnp.dot(features, w_both, preferred_element_type=jnp.float32).astype(jnp.bfloat16)
    key_values = lax.all_gather(local_kv, "band", axis=0, tiled=True)
    from_upper = passed_along(slots[0], "sector", -1)
    from_lower = passed_along(slots[2], "sector", 1)
    query_groups = jnp.stack([from_upper, slots[1], from_lower], axis=0)
    kv_groups = key_values.reshape(1, key_values.shape[0], 2 * model_width)
    results = attend_groups(query_groups, kv_groups)
    back_first = passed_along(results[0], "sector", 1)
    back_last = passed_along(results[2], "sector", -1)
    results = jnp.stack([back_first, results[1], back_last], axis=0)
    table = results.reshape(slot_total, model_width)
    picked = table[slot_codes].reshape(query_count, entries, model_width).astype(jnp.float32)
    mask_rows = live.reshape(query_count, entries, 1).astype(jnp.float32)
    summed = jnp.sum(picked * mask_rows, axis=1).astype(jnp.bfloat16)
    final = jnp.dot(summed, w_out, preferred_element_type=jnp.float32) + values_in
    return final.astype(jnp.bfloat16).reshape(azim_cells, range_cells, model_width)


def solution(mesh):
    return jax.shard_map(
        shards,
        mesh=mesh,
        in_specs=(
            P("sector", "band", None),
            P(),
            P(),
            P(),
            P(),
            P(),
            P(("sector", "band"), None),
            P("sector", "band", None),
            P("sector", "band", None),
        ),
        out_specs=P("sector", "band", None),
        check_vma=False,
    )
```

profile of v0, /device:TPU:1, one launch (start us, length us, event | category | flops | bytes accessed | tf_op | source)
XLA Modules:
  0.0 311.8 jit_solution(17708409824963561280)
XLA Ops:
  7.5 2.1 fusion.31
  15.6 2.6 reshape.155
  18.8 14.4 %scatter_custom_fusion = bf16[3072,256]{1,0:T(8,128)(2,1)S(1)} fusion(s32[3072]{0:T(1024)S(1)} %bitcast.139, bf16[3072,256]{1,0:T(8,128)(2,1)} %reshape.155, bf16[]{:T(256)} %constant.56.clone.1), kind=kCustom, calls=%fused_computation.54 | custom fusion | bytes 1573376 | tf_op jit(solution)/shard_map/scatter | solution.py:69
  34.2 7.3 %collective-permute-start = (bf16[8,128,256]{2,1,0:T(8,128)(2,1)S(1)}, bf16[8,128,256]{2,1,0:T(8,128)(2,1)}, u32[]{:S(2)}, u32[]{:S(2)}) collective-permute-start(bf16[8,128,256]{2,1,0:T(8,128)(2,1)S(1)} %bitcast.138), channel_id=1, source_target_pairs={{16,0},{32,16},{48,32},{64,48},{80,64},{96,80},{112,96},{128,112},... | collective-permute-start | bytes 1572872 | tf_op jit(solution)/shard_map/ppermute | solution.py:14
  43.1 53.2 %all-gather.2.cloned.1.call-done = bf16[8192,512]{0,1:T(8,128)(2,1)} async-done(((bf16[512,512]{0,1:T(8,128)(2,1)}), bf16[8192,512]{0,1:T(8,128)(2,1)}) %all-gather.2.cloned.1.call-update) | async-done | bytes 8388624 | tf_op jit(solution)/shard_map/all_gather | solution.py:74
  96.3 14.5 %reshape_reshape_squeeze_reshape.2 = bf16[4,2,1024,512]{2,1,0,3:T(2,128)(2,1)} reshape(bf16[8192,512]{0,1:T(8,128)(2,1)} %all-gather.2.cloned.1.call-done) | data formatting | bytes 16777216 | tf_op jit(solution)/shard_map/reshape;reshape;squeeze;reshape | solution.py:40
  110.8 11.3 %copy.18 = bf16[4,2,1024,512]{2,3,1,0:T(8,128)(2,1)} copy(bf16[4,2,1024,512]{2,1,0,3:T(2,128)(2,1)} %reshape_reshape_squeeze_reshape.2) | data formatting | bytes 16777216 | tf_op jit(solution)/shard_map/while | solution.py:41
  122.2 52.1 %while.30 = (s32[]{:T(128)}, bf16[4,2,128,256]{2,3,1,0:T(8,128)(2,1)S(1)}, bf16[4,2,1024,512]{2,3,1,0:T(8,128)(2,1)}, bf16[4,2,128,256]{3,2,1,0:T(8,128)(2,1)}, s32[]{:T(128)}) while((s32[]{:T(128)}, bf16[4,2,128,256]{2,3,1,0:T(8,128)(2,1)S(1)}, bf16[4,2,1024,512]{2,3,1,0:T(8,128)(2,1)}, bf16[4,2,128,256]{3,2,1,0:T(8,128)(2,1)}, ...), condition=%wide.region_6.7_spmd, body=%wide.region_3.6_spmd.sunk | while | flops 278987776 | bytes 28328008 | solution.py:41
  122.2 1.8 dynamic-slice_bitcast_fusion.6
  125.2 5.0 %fusion.91 = (f32[2,8,128]{2,1,0:T(8,128)S(1)}, f32[2,8,128,1024]{3,2,1,0:T(8,128)}) fusion(bf16[2,128,8,32]{1,3,2,0:T(8,128)(2,1)S(1)} %bitcast.127, bf16[2,1024,8,32]{1,3,2,0:T(8,128)(2,1)S(1)} %bitcast.123), kind=kOutput, calls=%fused_computation.66.clone.1 | convolution fusion | flops 140510208 | bytes 9576448 | tf_op jit(solution)/shard_map/while/body/eval_jaxpr/sub | solution.py:28
  130.2 5.0 %fusion.92 = bf16[2,8,32,128]{3,2,1,0:T(8,128)(2,1)S(1)} fusion(bf16[2,1024,8,32]{1,3,2,0:T(8,128)(2,1)S(1)} %bitcast.120, f32[2,8,128,1024]{3,2,1,0:T(8,128)} %get-tuple-element.218, f32[2,8,128]{2,1,0:T(8,128)S(1)} %get-tuple-element.219), kind=kOutput, calls=%fused_computation.11.clone.1 | convolution fusion | flops 138477568 | bytes 9576448 | tf_op jit(solution)/shard_map/while/body/eval_jaxpr/bhmk,bkhd->bmhd/dot_general | solution.py:30
  135.2 1.8 dynamic-slice_bitcast_fusion.6
  138.2 5.0 %fusion.91 = (f32[2,8,128]{2,1,0:T(8,128)S(1)}, f32[2,8,128,1024]{3,2,1,0:T(8,128)}) fusion(bf16[2,128,8,32]{1,3,2,0:T(8,128)(2,1)S(1)} %bitcast.127, bf16[2,1024,8,32]{1,3,2,0:T(8,128)(2,1)S(1)} %bitcast.123), kind=kOutput, calls=%fused_computation.66.clone.1 | convolution fusion | flops 140510208 | bytes 9576448 | tf_op jit(solution)/shard_map/while/body/eval_jaxpr/sub | solution.py:28
  143.2 5.0 %fusion.92 = bf16[2,8,32,128]{3,2,1,0:T(8,128)(2,1)S(1)} fusion(bf16[2,1024,8,32]{1,3,2,0:T(8,128)(2,1)S(1)} %bitcast.120, f32[2,8,128,1024]{3,2,1,0:T(8,128)} %get-tuple-element.218, f32[2,8,128]{2,1,0:T(8,128)S(1)} %get-tuple-element.219), kind=kOutput, calls=%fused_computation.11.clone.1 | convolution fusion | flops 138477568 | bytes 9576448 | tf_op jit(solution)/shard_map/while/body/eval_jaxpr/bhmk,bkhd->bmhd/dot_general | solution.py:30
  148.2 1.8 dynamic-slice_bitcast_fusion.6
  151.2 5.0 %fusion.91 = (f32[2,8,128]{2,1,0:T(8,128)S(1)}, f32[2,8,128,1024]{3,2,1,0:T(8,128)}) fusion(bf16[2,128,8,32]{1,3,2,0:T(8,128)(2,1)S(1)} %bitcast.127, bf16[2,1024,8,32]{1,3,2,0:T(8,128)(2,1)S(1)} %bitcast.123), kind=kOutput, calls=%fused_computation.66.clone.1 | convolution fusion | flops 140510208 | bytes 9576448 | tf_op jit(solution)/shard_map/while/body/eval_jaxpr/sub | solution.py:28
  156.2 5.0 %fusion.92 = bf16[2,8,32,128]{3,2,1,0:T(8,128)(2,1)S(1)} fusion(bf16[2,1024,8,32]{1,3,2,0:T(8,128)(2,1)S(1)} %bitcast.120, f32[2,8,128,1024]{3,2,1,0:T(8,128)} %get-tuple-element.218, f32[2,8,128]{2,1,0:T(8,128)S(1)} %get-tuple-element.219), kind=kOutput, calls=%fused_computation.11.clone.1 | convolution fusion | flops 138477568 | bytes 9576448 | tf_op jit(solution)/shard_map/while/body/eval_jaxpr/bhmk,bkhd->bmhd/dot_general | solution.py:30
  161.3 1.8 dynamic-slice_bitcast_fusion.6
  164.3 5.0 %fusion.91 = (f32[2,8,128]{2,1,0:T(8,128)S(1)}, f32[2,8,128,1024]{3,2,1,0:T(8,128)}) fusion(bf16[2,128,8,32]{1,3,2,0:T(8,128)(2,1)S(1)} %bitcast.127, bf16[2,1024,8,32]{1,3,2,0:T(8,128)(2,1)S(1)} %bitcast.123), kind=kOutput, calls=%fused_computation.66.clone.1 | convolution fusion | flops 140510208 | bytes 9576448 | tf_op jit(solution)/shard_map/while/body/eval_jaxpr/sub | solution.py:28
  169.3 5.0 %fusion.92 = bf16[2,8,32,128]{3,2,1,0:T(8,128)(2,1)S(1)} fusion(bf16[2,1024,8,32]{1,3,2,0:T(8,128)(2,1)S(1)} %bitcast.120, f32[2,8,128,1024]{3,2,1,0:T(8,128)} %get-tuple-element.218, f32[2,8,128]{2,1,0:T(8,128)S(1)} %get-tuple-element.219), kind=kOutput, calls=%fused_computation.11.clone.1 | convolution fusion | flops 138477568 | bytes 9576448 | tf_op jit(solution)/shard_map/while/body/eval_jaxpr/bhmk,bkhd->bmhd/dot_general | solution.py:30
  176.7 52.1 %while.32 = (s32[]{:T(128)}, bf16[4,2,128,256]{2,3,1,0:T(8,128)(2,1)S(1)}, bf16[4,2,1024,512]{2,3,1,0:T(8,128)(2,1)}, bf16[4,2,128,256]{3,2,1,0:T(8,128)(2,1)}, s32[]{:T(128)}) while((s32[]{:T(128)}, bf16[4,2,128,256]{2,3,1,0:T(8,128)(2,1)S(1)}, bf16[4,2,1024,512]{2,3,1,0:T(8,128)(2,1)}, bf16[4,2,128,256]{3,2,1,0:T(8,128)(2,1)}, ...), condition=%wide.region_14.15_spmd, body=%wide.region_11.14_spmd.sunk | while | flops 278987776 | bytes 28328008 | solution.py:41
  176.7 1.8 dynamic-slice_bitcast_fusion.8
  179.7 5.0 %fusion.103 = (f32[2,8,128]{2,1,0:T(8,128)S(1)}, f32[2,8,128,1024]{3,2,1,0:T(8,128)}) fusion(bf16[2,128,8,32]{1,3,2,0:T(8,128)(2,1)S(1)} %bitcast.129, bf16[2,1024,8,32]{1,3,2,0:T(8,128)(2,1)S(1)} %bitcast.124), kind=kOutput, calls=%fused_computation.70.clone.1 | convolution fusion | flops 140510208 | bytes 9576448 | tf_op jit(solution)/shard_map/while/body/eval_jaxpr/sub | solution.py:28
  184.7 5.0 %fusion.104 = bf16[2,8,32,128]{3,2,1,0:T(8,128)(2,1)S(1)} fusion(bf16[2,1024,8,32]{1,3,2,0:T(8,128)(2,1)S(1)} %bitcast.121, f32[2,8,128,1024]{3,2,1,0:T(8,128)} %get-tuple-element.234, f32[2,8,128]{2,1,0:T(8,128)S(1)} %get-tuple-element.235), kind=kOutput, calls=%fused_computation.37.clone.1 | convolution fusion | flops 138477568 | bytes 9576448 | tf_op jit(solution)/shard_map/while/body/eval_jaxpr/bhmk,bkhd->bmhd/dot_general | solution.py:30
  189.7 1.8 dynamic-slice_bitcast_fusion.8
  192.7 5.0 %fusion.103 = (f32[2,8,128]{2,1,0:T(8,128)S(1)}, f32[2,8,128,1024]{3,2,1,0:T(8,128)}) fusion(bf16[2,128,8,32]{1,3,2,0:T(8,128)(2,1)S(1)} %bitcast.129, bf16[2,1024,8,32]{1,3,2,0:T(8,128)(2,1)S(1)} %bitcast.124), kind=kOutput, calls=%fused_computation.70.clone.1 | convolution fusion | flops 140510208 | bytes 9576448 | tf_op jit(solution)/shard_map/while/body/eval_jaxpr/sub | solution.py:28
  197.7 5.0 %fusion.104 = bf16[2,8,32,128]{3,2,1,0:T(8,128)(2,1)S(1)} fusion(bf16[2,1024,8,32]{1,3,2,0:T(8,128)(2,1)S(1)} %bitcast.121, f32[2,8,128,1024]{3,2,1,0:T(8,128)} %get-tuple-element.234, f32[2,8,128]{2,1,0:T(8,128)S(1)} %get-tuple-element.235), kind=kOutput, calls=%fused_computation.37.clone.1 | convolution fusion | flops 138477568 | bytes 9576448 | tf_op jit(solution)/shard_map/while/body/eval_jaxpr/bhmk,bkhd->bmhd/dot_general | solution.py:30
  202.8 1.8 dynamic-slice_bitcast_fusion.8
  205.8 5.0 %fusion.103 = (f32[2,8,128]{2,1,0:T(8,128)S(1)}, f32[2,8,128,1024]{3,2,1,0:T(8,128)}) fusion(bf16[2,128,8,32]{1,3,2,0:T(8,128)(2,1)S(1)} %bitcast.129, bf16[2,1024,8,32]{1,3,2,0:T(8,128)(2,1)S(1)} %bitcast.124), kind=kOutput, calls=%fused_computation.70.clone.1 | convolution fusion | flops 140510208 | bytes 9576448 | tf_op jit(solution)/shard_map/while/body/eval_jaxpr/sub | solution.py:28
  210.8 5.0 %fusion.104 = bf16[2,8,32,128]{3,2,1,0:T(8,128)(2,1)S(1)} fusion(bf16[2,1024,8,32]{1,3,2,0:T(8,128)(2,1)S(1)} %bitcast.121, f32[2,8,128,1024]{3,2,1,0:T(8,128)} %get-tuple-element.234, f32[2,8,128]{2,1,0:T(8,128)S(1)} %get-tuple-element.235), kind=kOutput, calls=%fused_computation.37.clone.1 | convolution fusion | flops 138477568 | bytes 9576448 | tf_op jit(solution)/shard_map/while/body/eval_jaxpr/bhmk,bkhd->bmhd/dot_general | solution.py:30
  215.8 1.8 dynamic-slice_bitcast_fusion.8
  218.8 5.0 %fusion.103 = (f32[2,8,128]{2,1,0:T(8,128)S(1)}, f32[2,8,128,1024]{3,2,1,0:T(8,128)}) fusion(bf16[2,128,8,32]{1,3,2,0:T(8,128)(2,1)S(1)} %bitcast.129, bf16[2,1024,8,32]{1,3,2,0:T(8,128)(2,1)S(1)} %bitcast.124), kind=kOutput, calls=%fused_computation.70.clone.1 | convolution fusion | flops 140510208 | bytes 9576448 | tf_op jit(solution)/shard_map/while/body/eval_jaxpr/sub | solution.py:28
  223.8 5.0 %fusion.104 = bf16[2,8,32,128]{3,2,1,0:T(8,128)(2,1)S(1)} fusion(bf16[2,1024,8,32]{1,3,2,0:T(8,128)(2,1)S(1)} %bitcast.121, f32[2,8,128,1024]{3,2,1,0:T(8,128)} %get-tuple-element.234, f32[2,8,128]{2,1,0:T(8,128)S(1)} %get-tuple-element.235), kind=kOutput, calls=%fused_computation.37.clone.1 | convolution fusion | flops 138477568 | bytes 9576448 | tf_op jit(solution)/shard_map/while/body/eval_jaxpr/bhmk,bkhd->bmhd/dot_general | solution.py:30
  229.8 2.3 collective-permute-start.3
  232.2 48.5 %while.31 = (s32[]{:T(128)}, bf16[4,2,128,256]{2,3,1,0:T(8,128)(2,1)S(1)}, bf16[4,2,1024,512]{2,3,1,0:T(8,128)(2,1)}, bf16[4,2,128,256]{3,2,1,0:T(8,128)(2,1)S(1)}, s32[]{:T(128)}) while((s32[]{:T(128)}, bf16[4,2,128,256]{2,3,1,0:T(8,128)(2,1)S(1)}, bf16[4,2,1024,512]{2,3,1,0:T(8,128)(2,1)}, bf16[4,2,128,256]{3,2,1,0:T(8,128)(2,1)S(1)}, ...), condition=%wide.region_10.11_spmd, body=%wide.region_7.10_spmd.sunk | while | flops 278987776 | bytes 28328008 | solution.py:41
  232.2 1.8 dynamic-slice_bitcast_fusion.7
  234.3 5.0 %fusion.97 = (f32[2,8,128]{2,1,0:T(8,128)S(1)}, f32[2,8,128,1024]{3,2,1,0:T(8,128)}) fusion(bf16[2,128,8,32]{1,3,2,0:T(8,128)(2,1)S(1)} %bitcast.131, bf16[2,1024,8,32]{1,3,2,0:T(8,128)(2,1)S(1)} %bitcast.125), kind=kOutput, calls=%fused_computation.68.clone.1 | convolution fusion | flops 140510208 | bytes 9576448 | tf_op jit(solution)/shard_map/while/body/eval_jaxpr/sub | solution.py:28
  239.3 5.0 %fusion.98 = bf16[2,8,32,128]{3,2,1,0:T(8,128)(2,1)S(1)} fusion(bf16[2,1024,8,32]{1,3,2,0:T(8,128)(2,1)S(1)} %bitcast.122, f32[2,8,128,1024]{3,2,1,0:T(8,128)} %get-tuple-element.226, f32[2,8,128]{2,1,0:T(8,128)S(1)} %get-tuple-element.227), kind=kOutput, calls=%fused_computation.24.clone.1 | convolution fusion | flops 138477568 | bytes 9576448 | tf_op jit(solution)/shard_map/while/body/eval_jaxpr/bhmk,bkhd->bmhd/dot_general | solution.py:30
  244.3 1.8 dynamic-slice_bitcast_fusion.7
  246.4 5.0 %fusion.97 = (f32[2,8,128]{2,1,0:T(8,128)S(1)}, f32[2,8,128,1024]{3,2,1,0:T(8,128)}) fusion(bf16[2,128,8,32]{1,3,2,0:T(8,128)(2,1)S(1)} %bitcast.131, bf16[2,1024,8,32]{1,3,2,0:T(8,128)(2,1)S(1)} %bitcast.125), kind=kOutput, calls=%fused_computation.68.clone.1 | convolution fusion | flops 140510208 | bytes 9576448 | tf_op jit(solution)/shard_map/while/body/eval_jaxpr/sub | solution.py:28
  251.5 5.0 %fusion.98 = bf16[2,8,32,128]{3,2,1,0:T(8,128)(2,1)S(1)} fusion(bf16[2,1024,8,32]{1,3,2,0:T(8,128)(2,1)S(1)} %bitcast.122, f32[2,8,128,1024]{3,2,1,0:T(8,128)} %get-tuple-element.226, f32[2,8,128]{2,1,0:T(8,128)S(1)} %get-tuple-element.227), kind=kOutput, calls=%fused_computation.24.clone.1 | convolution fusion | flops 138477568 | bytes 9576448 | tf_op jit(solution)/shard_map/while/body/eval_jaxpr/bhmk,bkhd->bmhd/dot_general | solution.py:30
  258.6 5.0 %fusion.97 = (f32[2,8,128]{2,1,0:T(8,128)S(1)}, f32[2,8,128,1024]{3,2,1,0:T(8,128)}) fusion(bf16[2,128,8,32]{1,3,2,0:T(8,128)(2,1)S(1)} %bitcast.131, bf16[2,1024,8,32]{1,3,2,0:T(8,128)(2,1)S(1)} %bitcast.125), kind=kOutput, calls=%fused_computation.68.clone.1 | convolution fusion | flops 140510208 | bytes 9576448 | tf_op jit(solution)/shard_map/while/body/eval_jaxpr/sub | solution.py:28
  263.6 5.0 %fusion.98 = bf16[2,8,32,128]{3,2,1,0:T(8,128)(2,1)S(1)} fusion(bf16[2,1024,8,32]{1,3,2,0:T(8,128)(2,1)S(1)} %bitcast.122, f32[2,8,128,1024]{3,2,1,0:T(8,128)} %get-tuple-element.226, f32[2,8,128]{2,1,0:T(8,128)S(1)} %get-tuple-element.227), kind=kOutput, calls=%fused_computation.24.clone.1 | convolution fusion | flops 138477568 | bytes 9576448 | tf_op jit(solution)/shard_map/while/body/eval_jaxpr/bhmk,bkhd->bmhd/dot_general | solution.py:30
  270.7 5.0 %fusion.97 = (f32[2,8,128]{2,1,0:T(8,128)S(1)}, f32[2,8,128,1024]{3,2,1,0:T(8,128)}) fusion(bf16[2,128,8,32]{1,3,2,0:T(8,128)(2,1)S(1)} %bitcast.131, bf16[2,1024,8,32]{1,3,2,0:T(8,128)(2,1)S(1)} %bitcast.125), kind=kOutput, calls=%fused_computation.68.clone.1 | convolution fusion | flops 140510208 | bytes 9576448 | tf_op jit(solution)/shard_map/while/body/eval_jaxpr/sub | solution.py:28
  275.7 5.0 %fusion.98 = bf16[2,8,32,128]{3,2,1,0:T(8,128)(2,1)S(1)} fusion(bf16[2,1024,8,32]{1,3,2,0:T(8,128)(2,1)S(1)} %bitcast.122, f32[2,8,128,1024]{3,2,1,0:T(8,128)} %get-tuple-element.226, f32[2,8,128]{2,1,0:T(8,128)S(1)} %get-tuple-element.227), kind=kOutput, calls=%fused_computation.24.clone.1 | convolution fusion | flops 138477568 | bytes 9576448 | tf_op jit(solution)/shard_map/while/body/eval_jaxpr/bhmk,bkhd->bmhd/dot_general | solution.py:30
  282.4 11.1 %gather_fusion = bf16[3072,256]{1,0:T(8,128)(2,1)S(1)} fusion(bf16[3072,256]{1,0:T(8,128)(2,1)S(1)} %bitcast.119, s32[3072]{0:T(1024)S(1)} %copy-done.5), kind=kCustom, calls=%fused_computation | custom fusion | bytes 3158016 | tf_op jit(solution)/shard_map/gather | solution.py:84
  293.5 3.1 reshape.142
  296.6 7.2 %multiply_reduce_fusion.3 = bf16[1024,256]{1,0:T(8,128)(2,1)S(1)} fusion(f32[1024,3,256]{2,1,0:T(4,128)} %reshape.142, f32[1024,3]{1,0:T(8,128)S(1)} %bitcast.134), kind=kLoop, calls=%fused_computation.41 | loop fusion | flops 1310720 | bytes 3682304 | tf_op jit(solution)/shard_map/reduce_sum | solution.py:86
  (98 shorter events, 31.2 us)
Async XLA Ops:
  6.5 1.0 copy-start
  6.5 89.8 %all-gather.2.cloned.1.call-start = ((), (), s32[]{:S(2)}) async-start(), calls=%async_computation | async-start | bytes 8912896 | tf_op jit(solution)/shard_map/all_gather | solution.py:74
  12.5 5.7 %copy-start.6 = (s32[16,64,3]{1,0,2:T(8,128)S(1)}, s32[16,64,3]{1,0,2:T(8,128)}, u32[]{:S(2)}) copy-start(s32[16,64,3]{1,0,2:T(8,128)} %param.22) | copy-start | bytes 36868
  15.6 25.9 %copy-start.7 = (s32[16,64,3]{1,0,2:T(8,128)S(1)}, s32[16,64,3]{1,0,2:T(8,128)}, u32[]{:S(2)}) copy-start(s32[16,64,3]{1,0,2:T(8,128)} %param.23) | copy-start | bytes 36868
  34.2 87.9 %collective-permute-start = (bf16[8,128,256]{2,1,0:T(8,128)(2,1)S(1)}, bf16[8,128,256]{2,1,0:T(8,128)(2,1)}, u32[]{:S(2)}, u32[]{:S(2)}) collective-permute-start(bf16[8,128,256]{2,1,0:T(8,128)(2,1)S(1)} %bitcast.138), channel_id=1, source_target_pairs={{16,0},{32,16},{48,32},{64,48},{80,64},{96,80},{112,96},{128,112},... | collective-permute-start | bytes 1572872 | tf_op jit(solution)/shard_map/ppermute | solution.py:14
  41.5 135.1 %collective-permute-start.2 = (bf16[8,128,256]{2,1,0:T(8,128)(2,1)}, bf16[8,128,256]{2,1,0:T(8,128)(2,1)}, u32[]{:S(2)}, u32[]{:S(2)}) collective-permute-start(bf16[8,128,256]{2,1,0:T(8,128)(2,1)} %bitcast.27), channel_id=1, source_target_pairs={{240,0},{0,16},{16,32},{32,48},{48,64},{64,80},{80,96},{96,112},{1... | collective-permute-start | bytes 1572872 | tf_op jit(solution)/shard_map/ppermute | solution.py:14
  175.3 105.7 %collective-permute-start.1 = (bf16[8,128,256]{2,1,0:T(8,128)(2,1)}, bf16[8,128,256]{2,1,0:T(8,128)(2,1)}, u32[]{:S(2)}, u32[]{:S(2)}) collective-permute-start(bf16[8,128,256]{2,1,0:T(8,128)(2,1)} %copy.20), channel_id=1, source_target_pairs={{240,0},{0,16},{16,32},{32,48},{48,64},{64,80},{80,96},{96,112},{1... | collective-permute-start | bytes 1572872 | tf_op jit(solution)/shard_map/ppermute | solution.py:14
  229.8 51.2 %collective-permute-start.3 = (bf16[8,128,256]{2,1,0:T(8,128)(2,1)}, bf16[8,128,256]{2,1,0:T(8,128)(2,1)}, u32[]{:S(2)}, u32[]{:S(2)}) collective-permute-start(bf16[8,128,256]{2,1,0:T(8,128)(2,1)} %copy.25), channel_id=1, source_target_pairs={{16,0},{32,16},{48,32},{64,48},{80,64},{96,80},{112,96},{128,112},... | collective-permute-start | bytes 1572872 | tf_op jit(solution)/shard_map/ppermute | solution.py:14
  280.7 1.6 copy-start.5
  293.4 3.1 %copy-start.3 = (f32[16,64,3]{2,1,0:T(8,128)S(1)}, f32[16,64,3]{2,1,0:T(8,128)}, u32[]{:S(2)}) copy-start(f32[16,64,3]{2,1,0:T(8,128)} %copy.28) | copy-start | bytes 36868
  293.5 10.4 %copy-start.2 = (bf16[16,64,256]{2,1,0:T(8,128)(2,1)S(1)}, bf16[16,64,256]{2,1,0:T(8,128)(2,1)}, u32[]{:S(2)}) copy-start(bf16[16,64,256]{2,1,0:T(8,128)(2,1)} %param.15) | copy-start | bytes 1572868
  293.5 10.4 %copy-start.4 = (bf16[256,256]{1,0:T(8,128)(2,1)S(1)}, bf16[256,256]{1,0:T(8,128)(2,1)}, u32[]{:S(2)}) copy-start(bf16[256,256]{1,0:T(8,128)(2,1)} %param.20) | copy-start | bytes 393220
  293.5 11.4 %copy-start.1 = (bf16[512,256]{1,0:T(8,128)(2,1)S(1)}, bf16[512,256]{1,0:T(8,128)(2,1)}, u32[]{:S(2)}) copy-start(bf16[512,256]{1,0:T(8,128)(2,1)} %param.21) | copy-start | bytes 786436
Sparse Core Ops, SparseCore 0:
  9.9 86.3 all-gather.1
where the time goes:
time: 313 us; the launch traced here: 312 us
  matrix products  124 us (40%)
  local copies, waits for them, and re-layouts  96.1 us (31%)
  waiting for transfers between devices  53.2 us (17%)
  between operations  13.6 us (4%)
  other arithmetic  13.3 us (4%)
  starting transfers between devices  10.9 us (3%)
    sub x12, matrix products, attend_pair(): expo = jnp.exp(scores - peak)  60.1 us
    dot_general x12, matrix products, attend_pair(): jnp.einsum('bhmk,bkhd->bmhd', weights, value_heads, preferred_element_typ...  59.7 us
    all_gather x1, waiting for transfers between devices, shards(): key_values = lax.all_gather(local_kv, 'band', axis=0, tiled=True)  53.2 us
    squeeze x12, local copies, waits for them, and re-layouts, attend_many(): lax.map(lambda pair: attend_pair(pair[0], pair[1]), (grouped_rows, groupe...  21.2 us
    another operation x1, local copies, waits for them, and re-layouts, attend_many(): blocks.reshape((block_count // pair_size, pair_size) + blocks.shape[1:])  14.5 us
    scatter x1, local copies, waits for them, and re-layouts, shards(): slots = jnp.zeros((slot_total, model_width), jnp.bfloat16).at[slot_codes]...  14.4 us
    while x1, local copies, waits for them, and re-layouts, attend_many(): lax.map(lambda pair: attend_pair(pair[0], pair[1]), (grouped_rows, groupe...  11.3 us
    gather x1, local copies, waits for them, and re-layouts, shards(): table[slot_codes].reshape(query_count, entries, model_width)  11.1 us
  transfers between devices with their start and end apart: 5, of which 1 were waited for; matrix products, arithmetic and copies ran while one was open for 66% of the time, Pallas kernels for 0%

commit v1 on v0

v1 whole, which is shorter than its diff:
```python
import math

import jax
import jax.numpy as jnp
from jax import lax
from jax.experimental import pallas as pl
from jax.experimental.pallas import tpu as pltpu
from jax.sharding import PartitionSpec as P

HEADS = 8
BLK_DEV = 8
CAP = 128
N_SECTOR = 16
F32 = jnp.float32
BF16 = jnp.bfloat16
MESH = pl.DeviceIdType.MESH
LANES = 128
ROWS = 64


def kernel(
    queries, norm_gain, w_query, w_key, w_value, w_out, features, visible, live, out,
    proj, code_cols, code_rows, slots, qbuf, results, table, feats, relay, k_t, v_one, acc,
    f_send, f_recv, x_send, x_recv, g_send, q_send, q_recv, r_send, r_recv,
):
    azim, ranges, width = queries.shape
    query_count = azim * ranges
    entries = visible.shape[2]
    half, keys = features.shape[0], 2 * features.shape[0]
    head_size = width // HEADS
    scale = math.log2(math.e) * head_size ** -0.5
    nh = LANES // head_size

    s, j = lax.axis_index("sector"), lax.axis_index("band")
    x, y, c = j // 8, (j // 2) % 4, j % 2
    parity = y % 2
    away = (y + c) % 2

    def band(xx, yy, cc):
        return xx * 8 + yy * 2 + cc

    def sector(offset):
        return (s + offset + N_SECTOR) % N_SECTOR

    y_up, y_down = (y + 1) % 4, (y + 3) % 4
    other = (c + 1) % 2
    x_far = (x + 1) % 2

    barrier = pltpu.get_barrier_semaphore()
    greeted = [(s, band(x, y, other)), (s, band(x_far, y, c))]
    greeted += [(s, band(x, yy, cc)) for yy in (y_up, y_down) for cc in (0, 1)]
    greeted += [(sector(o), band(x, y, cc)) for o in (-1, 1) for cc in (0, 1)]
    for device in greeted:
        pl.semaphore_signal(barrier, inc=1, device_id=device, device_id_type=MESH)

    values_in = queries[...].reshape(query_count, width).astype(F32)
    average = jnp.mean(values_in, axis=-1, keepdims=True)
    spread = jnp.mean((values_in - average) ** 2, axis=-1, keepdims=True)
    normed = ((values_in - average) * lax.rsqrt(spread + 1e-05) * norm_gain[...]).astype(BF16)
    proj[...] = jnp.dot(normed, w_query[...], preferred_element_type=F32).astype(BF16)

    def remote(src, dst, send, recv, device):
        return pltpu.make_async_remote_copy(
            src_ref=src, dst_ref=dst, send_sem=send, recv_sem=recv, device_id=device, device_id_type=MESH
        )

    def local_of(xx, yy):
        return xx * 2 + yy // 2

    def spread_copies(src, xx, row):
        li = local_of(xx, y)
        up = remote(src, feats.at[li, c], f_send.at[row, 0], f_recv.at[li, c], (s, band(x, y_up, parity)))
        down = remote(src, feats.at[li, c], f_send.at[row, 1], f_recv.at[li, c], (s, band(x, y_down, parity)))
        across = remote(src, feats.at[li, c], f_send.at[row, 2], f_recv.at[li, c], (s, band(x, y, other)))
        stay = pltpu.make_async_copy(src, feats.at[li, c], f_recv.at[li, c])
        return up, down, across, stay

    def spread_start(src, xx, row):
        up, down, across, stay = spread_copies(src, xx, row)

        @pl.when(away == 1)
        def _():
            across.start()

        @pl.when(away == 0)
        def _():
            stay.start()

        up.start()
        down.start()

    def spread_wait(src, xx, row):
        up, down, across, stay = spread_copies(src, xx, row)
        up.wait_send()
        down.wait_send()

        @pl.when(away == 1)
        def _():
            across.wait_send()

    def forward_copies(xx, row):
        low, high = local_of(xx, y_down), local_of(xx, y_up)
        up = remote(feats.at[low, 0], feats.at[low, 0], g_send.at[row, 0], f_recv.at[low, 0], (s, band(x, y_up, c)))
        down = remote(feats.at[high, 1], feats.at[high, 1], g_send.at[row, 1], f_recv.at[high, 1], (s, band(x, y_down, c)))
        return up, down

    exchange = remote(features, relay, x_send.at[0], x_recv.at[0], (s, band(x_far, y, c)))

    def step_block(k, core):
        yy = (y + (y + core) % 2 + 2 * (k % 2)) % 4
        xx = (x + k // 2) % 2
        return xx, yy

    def query_copy(k, o, d):
        core = (c + d) % 2
        xx, yy = step_block(k, core)
        b, li = xx * 4 + yy, local_of(xx, yy)
        if o == 1 and d == 0:
            return pltpu.make_async_copy(slots.at[o, b], qbuf.at[li, 2 * o + d], q_recv.at[li, 2 * o + d])
        return remote(
            slots.at[o, b], qbuf.at[li, 2 * o + d], q_send.at[k, 2 * o + d], q_recv.at[li, 2 * o + d],
            (sector(o - 1), band(x, y, core)),
        )

    def result_copy(k, o, d):
        xx, yy = step_block(k, c)
        b, li = xx * 4 + yy, local_of(xx, yy)
        if o == 1 and d == 0:
            return pltpu.make_async_copy(results.at[li, 2 * o + d], table.at[o, b], r_recv.at[o, b])
        return remote(
            results.at[li, 2 * o + d], table.at[o, b], r_send.at[k, 2 * o + d], r_recv.at[o, b],
            (sector(1 - o), band(x, y, (c + d) % 2)),
        )

    pl.semaphore_wait(barrier, len(greeted))
    exchange.start()
    spread_start(features, x, 0)

    codes = visible[...].reshape(query_count, entries).astype(F32)
    alive = live[...].reshape(query_count, entries)
    diagonal = lax.broadcasted_iota(jnp.int32, (CAP, LANES), 0) == lax.broadcasted_iota(jnp.int32, (CAP, LANES), 1)
    lived = jnp.where(alive == 1, codes, -1.0)
    for t in range(entries):
        code_cols[t] = jnp.broadcast_to(lived[:, t : t + 1], (query_count, LANES))
        spread_code = jnp.broadcast_to(codes[:, t : t + 1], (query_count, LANES))
        for n in range(query_count // LANES):
            piece = spread_code[n * LANES : (n + 1) * LANES]
            code_rows[t : t + 1, n * LANES : (n + 1) * LANES] = jnp.sum(
                jnp.where(diagonal, piece, 0.0), axis=0, keepdims=True
            )

    slot_index = lax.broadcasted_iota(jnp.int32, (CAP, query_count), 0).astype(F32)

    @pl.loop(0, 4)
    def _(k):
        for d in (0, 1):
            xx, yy = step_block(k, (c + d) % 2)
            b = xx * 4 + yy
            picks = []
            for o in range(3):
                base = ((o * BLK_DEV + b) * CAP).astype(F32)
                hit = slot_index == (code_rows[0:1, :] - base)
                for t in range(1, entries):
                    hit = hit | (slot_index == (code_rows[t : t + 1, :] - base))
                picks.append(jnp.where(hit, 1.0, 0.0).astype(BF16))
            picked = jnp.dot(jnp.concatenate(picks, axis=0), proj[...], preferred_element_type=F32).astype(BF16)
            for o in range(3):
                slots[o, b] = picked[o * CAP : (o + 1) * CAP]
            for o in (0, 2, 1):
                query_copy(k, o, d).start()

    for t in range(2):
        v_one[t, :, LANES:] = jnp.ones((keys, LANES), BF16)
    w_key_t = w_key[...].T
    head = lax.broadcasted_iota(jnp.int32, (ROWS, LANES), 1) // head_size

    @pl.loop(0, 4)
    def _(k):
        xx, yy = step_block(k, c)
        li = local_of(xx, yy)

        @pl.when((away == 1) & (k % 2 == 0))
        def _():
            for yn in (y_down, y_up):
                for h in (0, 1):
                    here = feats.at[local_of(xx, yn), h]
                    pltpu.make_async_copy(here, here, f_recv.at[local_of(xx, yn), h]).wait()
            for copy in forward_copies(xx, k // 2):
                copy.start()

        @pl.when(away == 0)
        def _():
            for h in (0, 1):
                here = feats.at[li, h]
                pltpu.make_async_copy(here, here, f_recv.at[li, h]).wait()

        @pl.when(k == 1)
        def _():
            exchange.wait_recv()
            spread_start(relay, x_far, 1)

        tokens = feats[li].reshape(keys, width)
        k_t[...] = lax.dot_general(
            w_key_t, tokens, (((1,), (1,)), ((), ())), preferred_element_type=F32
        ).astype(BF16)
        value = jnp.dot(tokens, w_value[...], preferred_element_type=F32).astype(BF16)
        for t in range(2):
            v_one[t, :, :LANES] = value[:, t * LANES : (t + 1) * LANES]

        for o in range(3):
            for d in (0, 1):
                here = qbuf.at[li, 2 * o + d]
                pltpu.make_async_copy(here, here, q_recv.at[li, 2 * o + d]).wait()

        tiles = [(src, r0, t) for src in (0, 1, 4, 5, 2, 3) for r0 in range(0, CAP, ROWS) for t in range(2)]

        def scores_of(src, r0, t):
            rows = qbuf[li, src, r0 : r0 + ROWS, t * LANES : (t + 1) * LANES]
            stacked = jnp.concatenate([jnp.where(head == h, rows, jnp.zeros((), BF16)) for h in range(nh)], axis=0)
            return jnp.dot(stacked, k_t[t * LANES : (t + 1) * LANES, :], preferred_element_type=F32)

        scores = scores_of(*tiles[0])
        for i, (src, r0, t) in enumerate(tiles):
            later = scores_of(*tiles[i + 1]) if i + 1 < len(tiles) else None
            peak = jnp.max(scores, axis=1, keepdims=True)
            expo = jnp.exp2((scores - peak) * scale).astype(BF16)
            both = jnp.dot(expo, v_one[t], preferred_element_type=F32)
            parts = both[:, :LANES] / both[:, LANES:]
            merged = parts[:ROWS]
            for h in range(1, nh):
                merged = jnp.where(head == h, parts[h * ROWS : (h + 1) * ROWS], merged)
            results[li, src, r0 : r0 + ROWS, t * LANES : (t + 1) * LANES] = merged.astype(BF16)
            scores = later

        for o in (0, 2, 1):
            for d in (1, 0):
                result_copy(k, o, d).start()

    lane_index = lax.broadcasted_iota(jnp.int32, (query_count, LANES), 1).astype(F32)

    @pl.loop(0, 4)
    def _(k):
        masks, rows = [], []
        for d in (0, 1):
            xx, yy = step_block(k, (c + d) % 2)
            b = xx * 4 + yy
            for o in range(3):
                here = table.at[o, b]
                pltpu.make_async_copy(here, here, r_recv.at[o, b]).wait()
                target = lane_index + ((o * BLK_DEV + b) * CAP).astype(F32)
                hit = code_cols[0] == target
                for t in range(1, entries):
                    hit = hit | (code_cols[t] == target)
                masks.append(jnp.where(hit, 1.0, 0.0).astype(BF16))
                rows.append(table[o, b])
        part = jnp.dot(jnp.concatenate(masks, axis=1), jnp.concatenate(rows, axis=0), preferred_element_type=F32)

        @pl.when(k == 0)
        def _():
            acc[...] = part

        @pl.when(k > 0)
        def _():
            acc[...] += part

    summed = acc[...].astype(BF16)
    final = jnp.dot(summed, w_out[...], preferred_element_type=F32) + queries[...].reshape(query_count, width).astype(F32)
    out[...] = final.astype(BF16).reshape(azim, ranges, width)

    exchange.wait_send()
    spread_wait(features, x, 0)
    spread_wait(relay, x_far, 1)

    @pl.when(away == 1)
    def _():
        for row, xx in enumerate((x, x_far)):
            for copy in forward_copies(xx, row):
                copy.wait_send()

    @pl.loop(0, 4)
    def _(k):
        for o in range(3):
            for d in (0, 1):
                if not (o == 1 and d == 0):
                    query_copy(k, o, d).wait_send()
                    result_copy(k, o, d).wait_send()


def shards(queries, norm_gain, w_query, w_key, w_value, w_out, features, visible, live):
    azim, ranges, width = queries.shape
    query_count = azim * ranges
    half, keys = features.shape[0], 2 * features.shape[0]
    entries = visible.shape[2]
    dma = pltpu.SemaphoreType.DMA
    return pl.pallas_call(
        kernel,
        out_shape=jax.ShapeDtypeStruct(queries.shape, BF16),
        in_specs=[pl.BlockSpec(memory_space=pltpu.VMEM)] * 9,
        out_specs=pl.BlockSpec(memory_space=pltpu.VMEM),
        scratch_shapes=[
            pltpu.VMEM((query_count, width), BF16),
            pltpu.VMEM((entries, query_count, LANES), F32),
            pltpu.VMEM((8, query_count), F32),
            pltpu.VMEM((3, BLK_DEV, CAP, width), BF16),
            pltpu.VMEM((4, 6, CAP, width), BF16),
            pltpu.VMEM((4, 6, CAP, width), BF16),
            pltpu.VMEM((3, BLK_DEV, CAP, width), BF16),
            pltpu.VMEM((4, 2, half, width), BF16),
            pltpu.VMEM((half, width), BF16),
            pltpu.VMEM((width, keys), BF16),
            pltpu.VMEM((2, keys, 2 * LANES), BF16),
            pltpu.VMEM((query_count, width), F32),
            dma((2, 3)), dma((4, 2)), dma((1,)), dma((1,)), dma((2, 2)),
            dma((4, 6)), dma((4, 6)), dma((4, 6)), dma((3, BLK_DEV)),
        ],
        compiler_params=pltpu.CompilerParams(
            collective_id=0, has_side_effects=True, vmem_limit_bytes=56 * 2**20
        ),
    )(queries, norm_gain.reshape(1, -1), w_query, w_key, w_value, w_out, features, visible, live)


def solution(mesh):
    return jax.shard_map(
        shards,
        mesh=mesh,
        in_specs=(
            P("sector", "band", None), P(), P(), P(), P(), P(),
            P(("sector", "band"), None),
            P("sector", "band", None), P("sector", "band", None),
        ),
        out_specs=P("sector", "band", None),
        check_vma=False,
    )
```

time: 313 us -> 72 us (0.23)
  matrix products: 124 us -> 0 us
  local copies, waits for them, and re-layouts: 96.1 us -> 4.7 us
  Pallas kernels: 0 us -> 67.1 us
  waiting for transfers between devices: 53.2 us -> 0 us
  between operations: 13.6 us -> 0.01 us
  other arithmetic: 13.3 us -> 0 us
  starting transfers between devices: 10.9 us -> 0 us
    pallas_call x0 -> x1, Pallas kernels: none -> 67.1 us  [shards(): pl.pallas_call(kernel, out_shape=jax.ShapeDtypeStruct(queries.shape, BF16...]
    dot_general x15 -> x0, matrix products: 64.1 us -> none  [the longest x12 59.7 us: attend_pair(): jnp.einsum('bhmk,bkhd->bmhd', weights, value_heads, preferred_element_typ...]
    sub x12 -> x0, matrix products: 60.1 us -> none  [attend_pair(): expo = jnp.exp(scores - peak)]
    all_gather x1 -> x0, waiting for transfers between devices: 53.2 us -> none  [shards(): key_values = lax.all_gather(local_kv, 'band', axis=0, tiled=True)]
    squeeze x12 -> x0, local copies, waits for them, and re-layouts: 21.2 us -> none  [attend_many(): lax.map(lambda pair: attend_pair(pair[0], pair[1]), (grouped_rows, groupe...]
    another operation x7 -> x0, local copies, waits for them, and re-layouts: 17 us -> none  [the longest x1 14.5 us: attend_many(): blocks.reshape((block_count // pair_size, pair_size) + blocks.shape[1:])]
    scatter x1 -> x0, local copies, waits for them, and re-layouts: 14.4 us -> none  [shards(): slots = jnp.zeros((slot_total, model_width), jnp.bfloat16).at[slot_codes]...]
    while x1 -> x0, local copies, waits for them, and re-layouts: 11.3 us -> none  [attend_many(): lax.map(lambda pair: attend_pair(pair[0], pair[1]), (grouped_rows, groupe...]
  transfers between devices with their start and end apart: 5 -> 0, of which waited for: 1 -> 0; matrix products, arithmetic and copies ran while one was open for 66% -> 0% of each run, Pallas kernels for 0% -> 0%
where the time goes in v1:
time: 72 us; the launch traced here: 71.8 us
  Pallas kernels  67.1 us (93%)
  local copies, waits for them, and re-layouts  4.7 us (7%)
    pallas_call x1, Pallas kernels, shards(): pl.pallas_call(kernel, out_shape=jax.ShapeDtypeStruct(queries.shape, BF16...  67.1 us
    unnamed x5, local copies, waits for them, and re-layouts  4.7 us

profile of v1, /device:TPU:1, one launch (start us, length us, event | category | flops | bytes accessed | tf_op | source)
XLA Modules:
  0.0 71.8 jit_solution(760903262895932523)
XLA Ops:
  0.0 0.0 copy-start
  0.0 1.8 %copy.10.visible = s32[16,64,3]{2,1,0:T(8,128)} copy(s32[16,64,3]{1,0,2:T(8,128)} %param.16) | data formatting | bytes 24576 | tf_op args[7]
  1.8 0.0 copy-done
  1.8 1.0 %copy.11.live = s32[16,64,3]{2,1,0:T(8,128)} copy(s32[16,64,3]{1,0,2:T(8,128)S(1)} %copy-done) | data formatting | bytes 24576 | tf_op args[8]
  2.8 67.1 %shard_map.91 = bf16[16,64,256]{2,1,0:T(8,128)(2,1)} custom-call(bf16[16,64,256]{2,1,0:T(8,128)(2,1)} %queries.1, f32[1,256]{1,0:T(1,128)} %bitcast.1, bf16[256,256]{1,0:T(8,128)(2,1)} %w_query.1, bf16[256,256]{1,0:T(8,128)(2,1)} %w_key.1, bf16[256,256]{1,0:T(8,128)(2,1)} %w_value.1, bf16[256,256]{1,0:T(8,128)(2,1)} %w_out.1, bf16[512,256]{1,0:T(8,128)(2,1)} %features.1, ...), custom_call_target="tpu_custom_call" | custom-call | tf_op jit(solution)/shard_map/pallas_call | solution.py:295
  69.9 1.9 %copy.13 = bf16[16,64,256]{2,1,0:T(8,128)(2,1)} copy(bf16[16,64,256]{2,1,0:T(8,128)(2,1)} %shard_map.91) | data formatting | bytes 1048576
Async XLA Ops:
  0.0 1.8 %copy-start = (s32[16,64,3]{1,0,2:T(8,128)S(1)}, s32[16,64,3]{1,0,2:T(8,128)}, u32[]{:S(2)}) copy-start(s32[16,64,3]{1,0,2:T(8,128)} %param.17) | copy-start | bytes 36868

commit v2 on v1

--- a/solution.py
+++ b/solution.py
@@ -20,7 +20,7 @@
 
 def kernel(
     queries, norm_gain, w_query, w_key, w_value, w_out, features, visible, live, out,
-    proj, code_cols, code_rows, slots, qbuf, results, table, feats, relay, k_t, v_one, acc,
+    proj, code_cols, code_rows, slots, qbuf, results, table, feats, relay, k_t, v_all, acc,
     f_send, f_recv, x_send, x_recv, g_send, q_send, q_recv, r_send, r_recv,
 ):
     azim, ranges, width = queries.shape
@@ -169,8 +169,6 @@
             for o in (0, 2, 1):
                 query_copy(k, o, d).start()
 
-    for t in range(2):
-        v_one[t, :, LANES:] = jnp.ones((keys, LANES), BF16)
     w_key_t = w_key[...].T
     head = lax.broadcasted_iota(jnp.int32, (ROWS, LANES), 1) // head_size
 
@@ -203,9 +201,7 @@
         k_t[...] = lax.dot_general(
             w_key_t, tokens, (((1,), (1,)), ((), ())), preferred_element_type=F32
         ).astype(BF16)
-        value = jnp.dot(tokens, w_value[...], preferred_element_type=F32).astype(BF16)
-        for t in range(2):
-            v_one[t, :, :LANES] = value[:, t * LANES : (t + 1) * LANES]
+        v_all[...] = jnp.dot(tokens, w_value[...], preferred_element_type=F32).astype(BF16)
 
         for o in range(3):
             for d in (0, 1):
@@ -219,18 +215,29 @@
             stacked = jnp.concatenate([jnp.where(head == h, rows, jnp.zeros((), BF16)) for h in range(nh)], axis=0)
             return jnp.dot(stacked, k_t[t * LANES : (t + 1) * LANES, :], preferred_element_type=F32)
 
-        scores = scores_of(*tiles[0])
-        for i, (src, r0, t) in enumerate(tiles):
-            later = scores_of(*tiles[i + 1]) if i + 1 < len(tiles) else None
+        def weights_of(scores):
             peak = jnp.max(scores, axis=1, keepdims=True)
-            expo = jnp.exp2((scores - peak) * scale).astype(BF16)
-            both = jnp.dot(expo, v_one[t], preferred_element_type=F32)
-            parts = both[:, :LANES] / both[:, LANES:]
+            chunk = keys // 4
+            expos = [jnp.exp2((scores[:, n * chunk : (n + 1) * chunk] - peak) * scale) for n in range(4)]
+            total = jnp.sum((expos[0] + expos[1]) + (expos[2] + expos[3]), axis=1, keepdims=True)
+            inverse = 1.0 / total
+            return jnp.concatenate([(expo * inverse).astype(BF16) for expo in expos], axis=1)
+
+        def finish(src, r0, t, weights):
+            parts = jnp.dot(weights, v_all[...], preferred_element_type=F32)[:, t * LANES : (t + 1) * LANES]
             merged = parts[:ROWS]
             for h in range(1, nh):
                 merged = jnp.where(head == h, parts[h * ROWS : (h + 1) * ROWS], merged)
             results[li, src, r0 : r0 + ROWS, t * LANES : (t + 1) * LANES] = merged.astype(BF16)
-            scores = later
+
+        scores, weights = scores_of(*tiles[0]), None
+        for i, (src, r0, t) in enumerate(tiles):
+            later = scores_of(*tiles[i + 1]) if i + 1 < len(tiles) else None
+            new_weights = weights_of(scores)
+            if i > 0:
+                finish(*tiles[i - 1], weights)
+            scores, weights = later, new_weights
+        finish(*tiles[-1], weights)
 
         for o in (0, 2, 1):
             for d in (1, 0):
@@ -308,7 +315,7 @@
             pltpu.VMEM((4, 2, half, width), BF16),
             pltpu.VMEM((half, width), BF16),
             pltpu.VMEM((width, keys), BF16),
-            pltpu.VMEM((2, keys, 2 * LANES), BF16),
+            pltpu.VMEM((keys, width), BF16),
             pltpu.VMEM((query_count, width), F32),
             dma((2, 3)), dma((4, 2)), dma((1,)), dma((1,)), dma((2, 2)),
             dma((4, 6)), dma((4, 6)), dma((4, 6)), dma((3, BLK_DEV)),

time: 72 us -> 71.7 us (level)
  no operation moved by 1% of the time
where the time goes in v2:
time: 71.7 us; the launch traced here: 71.3 us
  Pallas kernels  66.6 us (93%)
  local copies, waits for them, and re-layouts  4.7 us (7%)
    pallas_call x1, Pallas kernels, shards(): pl.pallas_call(kernel, out_shape=jax.ShapeDtypeStruct(queries.shape, BF16...  66.6 us
    unnamed x5, local copies, waits for them, and re-layouts  4.7 us

profile of v2, /device:TPU:1, one launch (start us, length us, event | category | flops | bytes accessed | tf_op | source)
XLA Modules:
  0.0 71.3 jit_solution(14851347871904181577)
XLA Ops:
  0.0 0.0 copy-start
  0.0 1.8 %copy.10.visible = s32[16,64,3]{2,1,0:T(8,128)} copy(s32[16,64,3]{1,0,2:T(8,128)} %param.16) | data formatting | bytes 24576 | tf_op args[7]
  1.8 0.0 copy-done
  1.8 1.0 %copy.11.live = s32[16,64,3]{2,1,0:T(8,128)} copy(s32[16,64,3]{1,0,2:T(8,128)S(1)} %copy-done) | data formatting | bytes 24576 | tf_op args[8]
  2.8 66.6 %shard_map.91 = bf16[16,64,256]{2,1,0:T(8,128)(2,1)} custom-call(bf16[16,64,256]{2,1,0:T(8,128)(2,1)} %queries.1, f32[1,256]{1,0:T(1,128)} %bitcast.1, bf16[256,256]{1,0:T(8,128)(2,1)} %w_query.1, bf16[256,256]{1,0:T(8,128)(2,1)} %w_key.1, bf16[256,256]{1,0:T(8,128)(2,1)} %w_value.1, bf16[256,256]{1,0:T(8,128)(2,1)} %w_out.1, bf16[512,256]{1,0:T(8,128)(2,1)} %features.1, ...), custom_call_target="tpu_custom_call" | custom-call | tf_op jit(solution)/shard_map/pallas_call | solution.py:302
  69.4 1.9 %copy.13 = bf16[16,64,256]{2,1,0:T(8,128)(2,1)} copy(bf16[16,64,256]{2,1,0:T(8,128)(2,1)} %shard_map.91) | data formatting | bytes 1048576
Async XLA Ops:
  0.0 1.8 %copy-start = (s32[16,64,3]{1,0,2:T(8,128)S(1)}, s32[16,64,3]{1,0,2:T(8,128)}, u32[]{:S(2)}) copy-start(s32[16,64,3]{1,0,2:T(8,128)} %param.17) | copy-start | bytes 36868
